TPU v7x, 32 devices: a whole 2x2x4 slice. The times are simulated.
32 devices in a mesh: region: 2 (over x), dev: 16 (over z, y, core).
Axes of the slice: x: 2, y: 2, z: 4, core: 2. Of those that a mesh axis runs over, the one named last changes fastest.
Arguments:
- positions: float32 [3, 128, 128], P(None, ('region', 'dev')), as said below
- charges: float32 [128, 128], P(('region', 'dev')), may hold values from -3 to 3
- types: int32 [128, 128], P(('region', 'dev')), may hold values from 0 to 5
- pairs: int32 [128, 13], P(('region', 'dev')), may hold values from -1 to 127, as said below
- owner_map: int32 [128], replicated, may hold values from 0 to 127, as said below
Outputs:
- born_radius: float32 [128, 128], P(('region', 'dev'))
- energy: float32 [128, 128], P(('region', 'dev'))
- forces: float32 [3, 128, 128], P(None, ('region', 'dev'))
- born_grad: float32 [128, 128], P(('region', 'dev'))
Inputs may be any that keep to these rules, and one draw needn't show every extreme that they name: `pairs`: row g lists cells next to block g's cell; -1 marks an empty slot. The block that owner_map gives for a listed cell differs from g and lies in g's region (blocks r * 64 to (r + 1) * 64 - 1) or in the next region. No pair of blocks is listed twice, in either order. `owner_map`: for each region r, a permutation of the cells r * 64 to (r + 1) * 64 - 1 onto the blocks with the same ids. `positions`: any two atoms are 1.5 or more apart.
All inputs are finite; a program needn't handle non-finite values.
Results may differ from a plain program's by a relative error of at most 0.0003.
Values sent between devices are 32-bit elements; how exact they have to be, the bound alone decides.
No kernel may reach another device: no remote copies, remote signals or barrier semaphores. Data moves between devices by JAX's collectives and lax.ppermute only.
A program may use at most 64 MiB of HBM per device.

v0:
```python
import functools

import jax
import jax.numpy as jnp
from jax import lax
from jax.experimental import pallas as pl
from jax.experimental.pallas import tpu as pltpu
from jax.sharding import PartitionSpec as P

type_radii = (1.2, 1.7, 1.55, 1.52, 1.85, 1.8)
type_scales = (0.85, 0.72, 0.79, 0.85, 0.86, 0.96)
radius_offset = 0.09
born_alpha = 1.0
born_beta = 0.8
born_gamma = 4.85
solvent_tau = 1.0 - 1.0 / 78.5

ROW_X, ROW_Y, ROW_Z, ROW_TYPE, ROW_CHARGE, ROW_PARTNER, ROW_COUNT = range(7)
WINDOW_X, WINDOW_Y, WINDOW_Z, WINDOW_SCALED, WINDOW_CHARGE, WINDOW_COUNT = range(6)
LANES = 128
SUBLANES = 8
STEP = 2
ENERGY_STEP = 4
CHUNK = 32
LIST_ROWS = 32
PARTNERS = 2
ITEMS = 8
EMPTY_SLOT = -1.0e6
FAR_AWAY = 1.0e15

scaled_values = [scale * (radius - radius_offset) for radius, scale in zip(type_radii, type_scales)]
short_range = 1.01 * max(
    max(scaled_values) - (min(type_radii) - radius_offset),
    (max(type_radii) - radius_offset) - min(scaled_values),
    0.5,
)


def window_regions(region_count):
    return (region_count, True) if region_count <= 3 else (3, False)


def exchange_axes():
    return ("region", "dev") if window_regions(lax.axis_size("region"))[1] else ("dev",)


def sent_directly(copies):
    return lax.all_to_all(copies, exchange_axes(), split_axis=0, concat_axis=0, tiled=True)


def twin_count(device_count):
    return 2 - device_count % 2


def sent_to_both_twins(copies):
    count = lax.axis_size("dev")
    twins = twin_count(count)
    axes = exchange_axes()
    regions = lax.axis_size(axes) // count
    alike = [list(reversed(range(parity, regions * count, twins))) for parity in range(twins)]
    here = lax.all_to_all(copies, axes, split_axis=0, concat_axis=0, axis_index_groups=alike, tiled=True)
    if twins == 1:
        return [here]
    return [here, lax.ppermute(here, "dev", [(i, i ^ 1) for i in range(count)])]


def with_other_regions(here):
    regions = lax.axis_size("region")
    if window_regions(regions)[1]:
        return here
    below = lax.ppermute(here, "region", [(i, i + 1) for i in range(regions - 1)])
    above = lax.ppermute(here, "region", [(i + 1, i) for i in range(regions - 1)])
    return jnp.concatenate([below, here, above], axis=0)


def by_type(types, table):
    value = jnp.full(types.shape, table[0], jnp.float32)
    for index in range(1, len(table)):
        value = jnp.where(types == index, jnp.float32(table[index]), value)
    return value


def type_fields(types):
    intrinsic = by_type(types, type_radii)
    rho = intrinsic - radius_offset
    return intrinsic, rho, by_type(types, type_scales) * rho


def turned(rows):
    count, width = rows.shape
    if count < LANES:
        rows = jnp.concatenate([rows, jnp.zeros((LANES - count, width), rows.dtype)], axis=0)
    return rows.T


def spread(columns, index):
    count = columns.shape[0]
    wide = jnp.broadcast_to(columns[:, index : index + 1], (count, LANES))
    return wide.reshape(count // SUBLANES, SUBLANES, LANES)


def row_of(ref, field, row):
    return ref[field, pl.ds(row, SUBLANES, stride=0), :][None]


def diagonal(groups, first_atom):
    shape = (groups, SUBLANES, LANES)
    row = lax.broadcasted_iota(jnp.int32, shape, 0) * SUBLANES + lax.broadcasted_iota(jnp.int32, shape, 1)
    return row + first_atom == lax.broadcasted_iota(jnp.int32, shape, 2)


def lane_total(array):
    return jnp.sum(array.reshape(-1, LANES), axis=1, keepdims=True)


def lane_sums(arrays, count):
    atoms = arrays[0].shape[0] * SUBLANES
    lane = lax.broadcasted_iota(jnp.int32, (atoms, LANES), 1)
    packed = jnp.zeros((atoms, LANES), jnp.float32)
    for index, array in enumerate(arrays):
        packed = jnp.where(lane == index, lane_total(array), packed)
    return packed.T[:count]


def fields_kernel(blocks, atoms, *refs):
    inputs, copies_ref, here, sems = refs[:5], refs[5], refs[6:11], refs[11]
    moves = [pltpu.make_async_copy(src, dst, sems.at[i]) for i, (src, dst) in enumerate(zip(inputs, here))]
    for move in moves:
        move.start()
    for move in moves:
        move.wait()
    positions_ref, types_ref, charges_ref, pairs_ref, owner_ref = here
    slot = lax.broadcasted_iota(jnp.int32, (1, atoms), 1)
    partners = []
    for block in range(blocks):
        row = jnp.full((1, atoms), EMPTY_SLOT, jnp.float32)
        for index in range(pairs_ref.shape[1]):
            cell = pairs_ref[block, index]
            partner = jnp.where(cell >= 0, owner_ref[jnp.maximum(cell, 0)] + 1, int(EMPTY_SLOT))
            row = jnp.where(slot == index, partner.astype(jnp.float32), row)
        partners.append(row)
    rows = [positions_ref[axis] for axis in range(3)]
    rows += [types_ref[...].astype(jnp.float32), charges_ref[...], jnp.concatenate(partners, axis=0)]
    for copy in range(copies_ref.shape[0]):
        for index, row in enumerate(rows):
            copies_ref[copy, index] = row


def descreen(squared, rho, scaled):
    inv_dist = lax.rsqrt(squared)
    share = scaled * inv_dist
    inner = 0.25 - share
    high = 0.25 + share
    low = jnp.maximum(rho * inv_dist, inner)
    inv_low = pltpu.reciprocal(low, approx=True)
    ratio = low * pltpu.reciprocal(high, approx=True)
    curve = (1.0 - ratio) + inner * (ratio - high * inv_low)
    return (inv_low * curve + 2.0 * jnp.log(ratio)) * inv_dist


def descreen_any(squared, rho, scaled):
    rho, scaled = 4.0 * rho, 4.0 * scaled
    inv_dist = lax.rsqrt(squared)
    distance = squared * inv_dist
    high = distance + scaled
    gap = distance - scaled
    low = jnp.maximum(rho, jnp.abs(gap))
    inv_low = 1.0 / low
    inv_high = 1.0 / high
    quarter = 0.25 * inv_dist
    curve = (squared - scaled * scaled) * quarter
    body = (0.5 * (inv_low - inv_high)) * (1.0 - (inv_low + inv_high) * curve)
    body = body + jnp.log(low * inv_high) * quarter
    body = body + jnp.where(rho < -gap, 1.0 / rho - inv_low, 0.0)
    return jnp.where(high > rho, 8.0 * body, 0.0)


def neighbour_lists(partner_ref, first_home, home_id, first_window, homes, slots, filler, table_ref):
    window = partner_ref.shape[0]
    tiles = [slice(start, start + LANES) for start in range(0, window, LANES)]
    depth = -(-slots // SUBLANES) * SUBLANES
    ids = jnp.concatenate([partner_ref[tile, :].T[:depth] for tile in tiles], axis=1)
    lists = turned(partner_ref[pl.ds(first_home, homes), :])[:depth]
    lane = lax.broadcasted_iota(jnp.int32, (depth, window), 1)
    lane_id = (lane + (first_window + 1)).astype(jnp.float32)
    rows = []
    for home in range(homes):
        own = (home_id + home + 1).astype(jnp.float32)
        linked = (ids == own) | (lane_id == lists[:, home : home + 1])
        rows.append(jnp.max(jnp.where(linked, 1.0, 0.0), axis=0, keepdims=True))
    linked = jnp.concatenate(rows, axis=0)
    before = lax.broadcasted_iota(jnp.int32, (window, window), 0)
    after = lax.broadcasted_iota(jnp.int32, (window, window), 1)
    ramp = jnp.where(before <= after, 1.0, 0.0).astype(jnp.bfloat16)
    rank = jnp.dot(linked.astype(jnp.bfloat16), ramp, preferred_element_type=jnp.float32)
    place = jnp.where(linked > 0.0, rank, 0.0)
    total = jnp.sum(linked, axis=1, keepdims=True)
    name = lax.broadcasted_iota(jnp.int32, (LIST_ROWS, window), 1).astype(jnp.float32)
    spot = lax.broadcasted_iota(jnp.int32, (LIST_ROWS, window), 0).astype(jnp.float32)
    own_lane = lax.broadcasted_iota(jnp.int32, (LIST_ROWS, LANES), 1)

    def some_rows(start):
        first = jnp.asarray(start + 1).astype(jnp.float32)
        packed = jnp.zeros((LIST_ROWS, LANES), jnp.float32)
        for home in range(homes):
            hit = place[home : home + 1] == spot + first
            found = jnp.sum(jnp.where(hit, name - float(filler), 0.0), axis=1, keepdims=True)
            packed = jnp.where(own_lane == home, found, packed)
        rows = pl.ds(pl.multiple_of(SUBLANES + start, SUBLANES), LIST_ROWS)
        table_ref[rows, :] = packed.astype(jnp.int32) + filler

    counts = jnp.zeros((SUBLANES, LANES), jnp.float32)
    lane = lax.broadcasted_iota(jnp.int32, (SUBLANES, LANES), 1)
    for home in range(homes):
        counts = jnp.where(lane == home, total[home : home + 1], counts)
    longest = jnp.max(total)
    table_ref[0:SUBLANES, :] = jnp.where(lane == LANES - 1, longest, counts).astype(jnp.int32)
    some_rows(0)

    def more_rows(turn, carry):
        some_rows(turn * LIST_ROWS)
        return carry

    lax.fori_loop(1, (longest.astype(jnp.int32) + (LIST_ROWS - 1)) // LIST_ROWS, more_rows, 0)


def move_lists(table_ref, lists_ref, sem, when_wanted):
    usual = pl.ds(0, SUBLANES + LIST_ROWS)
    move = pltpu.make_async_copy(table_ref.at[usual], lists_ref.at[usual], sem)
    move.start()
    when_wanted()
    move.wait()
    rows = lists_ref.shape[0] - (SUBLANES + LIST_ROWS)
    if rows > 0:

        @pl.when(lists_ref[0, LANES - 1] > LIST_ROWS)
        def _():
            rest = pl.ds(SUBLANES + LIST_ROWS, rows)
            more = pltpu.make_async_copy(table_ref.at[rest], lists_ref.at[rest], sem)
            more.start()
            more.wait()


def device_place(blocks, parts, whole):
    region, device = lax.axis_index("region"), lax.axis_index("dev")
    region_blocks = lax.axis_size("dev") * blocks
    first_window = 0 if whole else (region - 1) * region_blocks
    first_own = region * region_blocks + device * blocks
    part = lax.rem(device, parts)
    return first_window, first_own - part * blocks, first_own, part


def radii_kernel(
    blocks,
    slots,
    twins,
    whole,
    order,
    *refs,
):
    arrived_refs, refs = refs[:twins], refs[twins:]
    copies_ref, table_ref, window_ref, columns_ref, types_ref, partner_ref, total_ref, *refs = refs
    turned_ref, packed_ref, near_ref, lists_ref, items_ref, lists_sem = refs
    _, homes, groups, _, _ = columns_ref.shape
    chunk = groups * SUBLANES
    window = types_ref.shape[0]
    parts = homes // blocks
    together = PARTNERS
    first_window, home_id, _, part = device_place(blocks, parts, whole)
    first_home = pl.multiple_of(home_id - first_window, homes)
    first_atom = pl.multiple_of(part * chunk, chunk)

    tables = [window_ref.at[WINDOW_X], window_ref.at[WINDOW_Y], window_ref.at[WINDOW_Z]]
    tables += [types_ref, window_ref.at[WINDOW_CHARGE], partner_ref]
    odd = lax.rem(lax.axis_index("dev"), 2) == 1
    for place, pair in enumerate(order):
        for field, table in enumerate(tables):
            rows = [ref[place, field * blocks : (field + 1) * blocks, :] for ref in arrived_refs]
            if twins == 2:
                rows = [jnp.where(odd, rows[1], rows[0]), jnp.where(odd, rows[0], rows[1])]
            first = pair * twins * blocks
            table[first : first + twins * blocks, :] = jnp.concatenate(rows, axis=0)
    if partner_ref.shape[0] > window:
        spare = (partner_ref.shape[0] - window, LANES)
        partner_ref[window:, :] = jnp.full(spare, EMPTY_SLOT, jnp.float32)
    def scaled_radii():
        _, _, scaled = type_fields(types_ref[...])
        window_ref[WINDOW_SCALED, 0:window, :] = 0.25 * scaled
        for field in range(WINDOW_COUNT):
            filler = FAR_AWAY if field == WINDOW_X else 0.0
            window_ref[field, window : window + SUBLANES, :] = jnp.full((SUBLANES, LANES), filler, jnp.float32)

    def home_columns():
        scaled_radii()
        home_rows = [window_ref[field, pl.ds(first_home, homes), :] for field in range(3)]
        turned_ref[...] = turned(jnp.concatenate([types_ref[pl.ds(first_home, homes), :]] + home_rows, axis=0))
        columns = turned_ref[pl.ds(first_atom, chunk), :]
        _, rho, _ = type_fields(columns)
        for home in range(homes):
            columns_ref[0, home] = spread(0.25 * rho, home)
            for index in range(1, 4):
                columns_ref[index, home] = spread(columns, index * homes + home)

    def pair_distance(home, step, rows):
        dx = columns_ref[1, home, step] - rows[0]
        dy = columns_ref[2, home, step] - rows[1]
        dz = columns_ref[3, home, step] - rows[2]
        return dx * dx + dy * dy + dz * dz

    steps = [pl.ds(start, STEP) for start in range(0, groups, STEP)]

    shift = lists_ref.shape[0].bit_length()
    usual = 16 // PARTNERS + 6

    def list_items(home, filled):
        turns = (lists_ref[0, home] + (together - 1)) // together

        def put(index, carry):
            items_ref[filled + index] = (home << shift) + index * together
            return carry

        for index in range(usual):
            put(index, 0)
        lax.fori_loop(usual, turns, put, 0)
        return filled + turns

    def own_sweep(integral):
        near_ref[...] = jnp.full(near_ref.shape, FAR_AWAY, jnp.float32)
        own_together = min(homes, 2 * LANES // chunk)

        def own_pairs(turn, carry):
            for index in range(own_together):
                home = turn * own_together + index
                rows = [row_of(window_ref, field, first_home + home) for field in range(4)]
                for start, step in zip(range(0, groups, STEP), steps):
                    same = diagonal(STEP, first_atom + start * SUBLANES)
                    squared = jnp.where(same, FAR_AWAY, pair_distance(home, step, rows))
                    term = integral(squared, columns_ref[0, home, step], rows[3])
                    total_ref[home, step] = jnp.where(same, 0.0, term)
                    near_ref[...] = jnp.minimum(near_ref[...], squared)
            return carry

        lax.fori_loop(0, homes // own_together, own_pairs, 0)

    def sweep(integral, item_count):
        def visit(turn, nearest):
            sums = []
            for index in range(ITEMS):
                item = items_ref[turn * ITEMS + index]
                line, entry = item >> shift, item & ((1 << shift) - 1)
                home = jnp.minimum(line, homes - 1)
                parts_of = [None] * len(steps)
                for other in range(together):
                    partner = lists_ref[SUBLANES + entry + other, line]
                    rows = [row_of(window_ref, field, partner) for field in range(4)]
                    for place, step in enumerate(steps):
                        squared = pair_distance(home, step, rows)
                        nearest = jnp.minimum(nearest, squared)
                        term = integral(squared, columns_ref[0, home, step], rows[3])
                        parts_of[place] = term if other == 0 else parts_of[place] + term
                sums.append((home, parts_of))
            for home, parts_of in sums:
                for part, step in zip(parts_of, steps):
                    total_ref[home, step] += part
            return nearest

        near_ref[...] = lax.fori_loop(0, (item_count + (ITEMS - 1)) // ITEMS, visit, near_ref[...])
        lane = lax.broadcasted_iota(jnp.int32, (chunk, LANES), 1)
        packed = jnp.zeros((chunk, LANES), jnp.float32)
        for home in range(homes):
            packed = jnp.where(lane == home, lane_total(total_ref[home]), packed)
        packed_ref[...] = packed

    def meanwhile():
        home_columns()
        own_sweep(descreen)

    neighbour_lists(partner_ref, first_home, home_id, first_window, homes, slots, window, table_ref)
    move_lists(table_ref, lists_ref, lists_sem, meanwhile)
    intrinsic, rho, _ = type_fields(turned_ref[pl.ds(first_atom, chunk), :])
    item_count = lax.fori_loop(0, homes, list_items, 0)
    for index in range(ITEMS):
        items_ref[item_count + index] = homes << shift
    sweep(descreen, item_count)

    @pl.when(jnp.min(near_ref[...]) < short_range * short_range)
    def _():
        own_sweep(descreen_any)
        sweep(descreen_any, item_count)

    psi = (0.125 * packed_ref[...]) * rho
    shaped = born_alpha * psi - born_beta * psi * psi + born_gamma * psi * psi * psi
    radii = 1.0 / (1.0 / rho - jnp.tanh(shaped) / intrinsic)

    if chunk < LANES:
        radii = jnp.concatenate([radii, jnp.zeros((LANES - chunk, LANES), jnp.float32)], axis=0)
    turned_ref[...] = radii.T
    lane = lax.broadcasted_iota(jnp.int32, (blocks, LANES), 1)
    sent = turned_ref[pl.ds(0, blocks, stride=parts), :]
    for index in range(1, parts):
        rows = pltpu.roll(turned_ref[pl.ds(index, blocks, stride=parts), :], index * chunk, 1)
        sent = jnp.where(lane >= index * chunk, rows, sent)
    for copy in range(copies_ref.shape[0]):
        copies_ref[copy] = sent


def energy_kernel(
    parts,
    whole,
    table_ref,
    window_ref,
    gathered_ref,
    own_radii_ref,
    energy_ref,
    forces_ref,
    grad_ref,
    columns_ref,
    radii_ref,
    total_ref,
    lists_ref,
    lists_sem,
):
    devices, blocks, atoms = gathered_ref.shape
    window = devices * blocks
    part_rows = window // parts
    chunk = atoms // parts
    groups = atoms // SUBLANES
    first_window, _, own_id, part_here = device_place(blocks, parts, whole)
    first_own, list_lane = own_id - first_window, part_here * blocks
    fields = [(window_ref, field) for field in (WINDOW_X, WINDOW_Y, WINDOW_Z, WINDOW_CHARGE)] + [(radii_ref, 0)]

    def unpack():
        lane = lax.broadcasted_iota(jnp.int32, (part_rows, LANES), 1)
        pieces = [
            gathered_ref[pl.ds(part, devices // parts, stride=parts)].reshape(part_rows, atoms)
            for part in range(parts)
        ]
        for place in range(parts):
            whole_rows = pieces[0] if place == 0 else pltpu.roll(pieces[0], (parts - place) * chunk, 1)
            for part in range(1, parts):
                shift = (part - place) % parts
                piece = pieces[part] if shift == 0 else pltpu.roll(pieces[part], shift * chunk, 1)
                whole_rows = jnp.where(lane >= part * chunk, piece, whole_rows)
            radii_ref[0, pl.ds(place, part_rows, stride=parts), :] = whole_rows
        radii_ref[0, window : window + SUBLANES, :] = jnp.ones((SUBLANES, LANES), jnp.float32)

    def own_rows(ref, field):
        return jnp.concatenate([ref[field, pl.ds(first_own + block, 1), :] for block in range(blocks)], axis=0)

    def home_columns(block, start):
        return [columns_ref[field * blocks + block, pl.ds(start, ENERGY_STEP)] for field in range(4)]

    def pair_terms(home, rows, same=None):
        x, y, z, charge, radius = rows
        dx = home[0] - x
        dy = home[1] - y
        dz = home[2] - z
        squared = dx * dx + dy * dy + dz * dz
        if same is not None:
            squared = jnp.where(same, 1.0, squared)
            charge = jnp.where(same, 0.0, charge)
        spread_sq = home[3] * radius
        power = squared * pltpu.reciprocal(spread_sq, approx=True)
        quarter = 0.25 * jnp.exp(power)
        root_sq = squared - spread_sq * quarter
        inv_root = lax.rsqrt(root_sq)
        potential = charge * inv_root
        pull = (potential * pltpu.reciprocal(root_sq, approx=True)) * (1.0 - quarter)
        return (pull * dx, pull * dy, pull * dz, potential, pull * squared)

    def own_pairs():
        unpack()
        own_radii = own_rows(radii_ref, 0)
        own_radii_ref[...] = own_radii
        own = [own_rows(window_ref, field) for field in (WINDOW_X, WINDOW_Y, WINDOW_Z)]
        columns = turned(jnp.concatenate(own + [-4.0 * own_radii], axis=0))
        for index in range(4 * blocks):
            columns_ref[index] = spread(columns, index)
        for block in range(blocks):
            rows = [row_of(ref, field, first_own + block) for ref, field in fields]
            for start in range(0, groups, ENERGY_STEP):
                step = pl.ds(start, ENERGY_STEP)
                terms = pair_terms(home_columns(block, start), rows, diagonal(ENERGY_STEP, start * SUBLANES))
                for term, value in enumerate(terms):
                    total_ref[term * blocks + block, step] = value

    move_lists(table_ref, lists_ref, lists_sem, own_pairs)
    for block in range(blocks):

        def visit(count, first, index, carry, block=block):
            partners = []
            for other in range(count):
                partner = lists_ref[SUBLANES + first + index * count + other, list_lane + block]
                partners.append([row_of(ref, field, partner) for ref, field in fields])
            for start in range(0, groups, ENERGY_STEP):
                step = pl.ds(start, ENERGY_STEP)
                home = home_columns(block, start)
                sums = [total_ref[term * blocks + block, step] for term in range(5)]
                for rows in partners:
                    sums = [total + value for total, value in zip(sums, pair_terms(home, rows))]
                for term, value in enumerate(sums):
                    total_ref[term * blocks + block, step] = value
            return carry

        left = lists_ref[0, list_lane + block]
        first = 0
        for count in (4, 2, 1):
            turns = left // count
            lax.fori_loop(0, turns, functools.partial(visit, count, first), 0)
            first = first + turns * count
            left = left - turns * count
    sums = lane_sums([total_ref[index] for index in range(5 * blocks)], 5 * blocks)
    charges = own_rows(window_ref, WINDOW_CHARGE)
    own_decay = 1.0 / own_radii_ref[...]
    scale = solvent_tau * charges
    for axis in range(3):
        forces_ref[axis] = -scale * sums[axis * blocks : (axis + 1) * blocks]
    own_energy = 0.5 * scale * charges * own_decay
    energy_ref[...] = -0.5 * scale * sums[3 * blocks : 4 * blocks] - own_energy
    radial = sums[3 * blocks : 4 * blocks] - sums[4 * blocks : 5 * blocks]
    grad_ref[...] = (own_energy + 0.5 * scale * radial) * own_decay


def shards(positions, charges, types, pairs, owner_map):
    _, blocks, atoms = positions.shape
    regions = lax.axis_size("region")
    region_devices = lax.axis_size("dev")
    kept_regions, whole = window_regions(regions)
    devices = kept_regions * region_devices
    window = devices * blocks
    parts = atoms // CHUNK
    while region_devices % parts or 4 * parts * blocks > LANES:
        parts //= 2
    homes = parts * blocks
    chunk = atoms // parts

    vmem = pl.BlockSpec(memory_space=pltpu.VMEM)
    params = pltpu.CompilerParams(vmem_limit_bytes=40 * 1024 * 1024)
    copy_count = lax.axis_size(exchange_axes())
    twins = twin_count(region_devices)
    arrived = sent_to_both_twins(
        pl.pallas_call(
            functools.partial(fields_kernel, blocks, atoms),
            out_shape=jax.ShapeDtypeStruct((copy_count // twins, ROW_COUNT, blocks, atoms), jnp.float32),
            in_specs=[pl.BlockSpec(memory_space=pltpu.HBM)] * 5,
            out_specs=vmem,
            scratch_shapes=[
                pltpu.VMEM(positions.shape, positions.dtype),
                pltpu.VMEM(types.shape, types.dtype),
                pltpu.VMEM(charges.shape, charges.dtype),
                pltpu.SMEM(pairs.shape, pairs.dtype),
                pltpu.SMEM(owner_map.shape, owner_map.dtype),
                pltpu.SemaphoreType.DMA((5,)),
            ],
        )(positions, types, charges, pairs, owner_map)
    )
    arrived = [with_other_regions(part).reshape(devices // twins, ROW_COUNT * blocks, atoms) for part in arrived]
    padded = -(-window // LANES) * LANES
    table = jax.ShapeDtypeStruct((SUBLANES + padded, LANES), jnp.int32)
    pairs_sent = copy_count // twins
    pair_order = [
        first + place for first in range(0, devices // twins, pairs_sent) for place in reversed(range(pairs_sent))
    ]
    fields = jax.ShapeDtypeStruct((WINDOW_COUNT, window + SUBLANES, atoms), jnp.float32)
    copies, lists, window_fields = pl.pallas_call(
        functools.partial(radii_kernel, blocks, pairs.shape[1], twins, whole, pair_order),
        out_shape=(jax.ShapeDtypeStruct((copy_count, blocks, atoms), jnp.float32), table, fields),
        in_specs=[vmem] * twins,
        out_specs=(vmem, vmem, vmem),
        scratch_shapes=[
            pltpu.VMEM((4, homes, chunk // SUBLANES, SUBLANES, LANES), jnp.float32),
            pltpu.VMEM((window, atoms), jnp.float32),
            pltpu.VMEM((padded, atoms), jnp.float32),
            pltpu.VMEM((homes, chunk // SUBLANES, SUBLANES, LANES), jnp.float32),
            pltpu.VMEM((LANES, LANES), jnp.float32),
            pltpu.VMEM((chunk, LANES), jnp.float32),
            pltpu.VMEM((STEP, SUBLANES, LANES), jnp.float32),
            pltpu.SMEM(table.shape, jnp.int32),
            pltpu.SMEM((homes * (padded // PARTNERS + 1) + 64,), jnp.int32),
            pltpu.SemaphoreType.DMA(()),
        ],
        compiler_params=params,
    )(*arrived)
    block_out = jax.ShapeDtypeStruct((blocks, atoms), jnp.float32)
    window_radii = with_other_regions(sent_directly(copies))
    own_radii, energy, forces, grad = pl.pallas_call(
        functools.partial(energy_kernel, parts, whole),
        out_shape=(block_out, block_out, jax.ShapeDtypeStruct((3, blocks, atoms), jnp.float32), block_out),
        in_specs=[pl.BlockSpec(memory_space=pl.ANY), vmem, vmem],
        out_specs=(vmem, vmem, vmem, vmem),
        scratch_shapes=[
            pltpu.VMEM((4 * blocks, atoms // SUBLANES, SUBLANES, LANES), jnp.float32),
            pltpu.VMEM((1, window + SUBLANES, atoms), jnp.float32),
            pltpu.VMEM((5 * blocks, atoms // SUBLANES, SUBLANES, LANES), jnp.float32),
            pltpu.SMEM(table.shape, jnp.int32),
            pltpu.SemaphoreType.DMA(()),
        ],
        compiler_params=params,
    )(lists, window_fields, window_radii)
    return own_radii, energy, forces, grad


def solution(mesh):
    placed = (
        P(None, ("region", "dev"), None),
        P(("region", "dev"), None),
        P(("region", "dev"), None),
        P(("region", "dev"), None),
        P(),
    )
    return jax.shard_map(
        shards,
        mesh=mesh,
        in_specs=placed,
        out_specs=(
            P(("region", "dev"), None),
            P(("region", "dev"), None),
            P(None, ("region", "dev"), None),
            P(("region", "dev"), None),
        ),
        check_vma=False,
    )
```

profile of v0, /device:TPU:0, one launch (start us, length us, event | category | flops | bytes accessed | tf_op | source)
XLA Modules:
  0.0 44.7 jit_solution(16794362832852046005)
XLA Ops:
  0.6 1.7 %shard_map.84 = f32[16,6,4,128]{3,2,1,0:T(4,128)} custom-call(f32[3,4,128]{2,1,0:T(4,128)} %refs_0_.1, s32[4,128]{1,0:T(4,128)} %refs_1_.1, f32[4,128]{1,0:T(4,128)} %refs_2_.1, s32[4,13]{1,0:T(4,128)} %refs_3_.1, s32[128]{0:T(128)} %refs_4_.1), custom_call_target="tpu_custom_call" | custom-call | tf_op jit(solution)/shard_map/pallas_call | solution.py:542
  2.3 15.3 %all_to_all.10 = f32[16,6,4,128]{3,2,1,0:T(4,128)S(1)} all-to-all(f32[16,6,4,128]{3,2,1,0:T(4,128)} %shard_map.84), channel_id=1, replica_groups={{30,28,26,24,22,20,18,16,14,12,10,8,6,4,2,0},{31,29,27,25,23,21,19,17,1..., dimensions={0} | all-to-all | bytes 393216 | tf_op jit(solution)/shard_map/all_to_all | solution.py:61
  17.7 0.0 collective-permute-start
  17.7 1.4 %collective-permute-done = f32[16,6,4,128]{3,2,1,0:T(4,128)S(1)} collective-permute-done((f32[16,6,4,128]{3,2,1,0:T(4,128)S(1)}, f32[16,6,4,128]{3,2,1,0:T(4,128)S(1)}, u32[]{:S(2)}, u32[]{:S(2)}) %collective-permute-start) | collective-permute-done | bytes 196640 | tf_op jit(solution)/shard_map/ppermute | solution.py:64
  19.1 7.2 %shard_map.85 = (f32[32,4,128]{2,1,0:T(4,128)S(1)}, s32[136,128]{1,0:T(8,128)S(1)}, f32[5,136,128]{2,1,0:T(8,128)S(1)}) custom-call(f32[16,24,128]{2,1,0:T(8,128)S(1)} %bitcast.2, f32[16,24,128]{2,1,0:T(8,128)S(1)} %bitcast.3), custom_call_target="tpu_custom_call" | custom-call | tf_op jit(solution)/shard_map/pallas_call | solution.py:565
  26.3 11.6 %all_to_all.11.gathered_ref = f32[32,4,128]{2,1,0:T(4,128)S(1)} all-to-all(f32[32,4,128]{2,1,0:T(4,128)S(1)} %get-tuple-element.9), channel_id=1, replica_groups=mesh['region'=2,'dev'=16] {'region','dev'}, dimensions={0} | all-to-all | bytes 131072 | tf_op jit(solution)/shard_map/all_to_all | solution.py:48
  37.9 6.8 %shard_map.86 = (f32[4,128]{1,0:T(4,128)}, f32[4,128]{1,0:T(4,128)}, f32[3,4,128]{2,1,0:T(4,128)}, f32[4,128]{1,0:T(4,128)}) custom-call(s32[136,128]{1,0:T(8,128)S(1)} %get-tuple-element.7.table_ref, f32[5,136,128]{2,1,0:T(8,128)S(1)} %get-tuple-element.8.window_ref, f32[32,4,128]{2,1,0:T(4,128)S(1)} %all_to_all.11.gathered_ref), custom_call_target="tpu_custom_call" | custom-call | tf_op jit(solution)/shard_map/pallas_call | solution.py:586
Async XLA Ops:
  17.7 1.4 %collective-permute-start = (f32[16,6,4,128]{3,2,1,0:T(4,128)S(1)}, f32[16,6,4,128]{3,2,1,0:T(4,128)S(1)}, u32[]{:S(2)}, u32[]{:S(2)}) collective-permute-start(f32[16,6,4,128]{3,2,1,0:T(4,128)S(1)} %all_to_all.10), channel_id=1, source_target_pairs={{0,1},{1,0},{2,3},{3,2},{4,5},{5,4},{6,7},{7,6},{8,9},{9,8},{10,11... | collective-permute-start | bytes 589832 | tf_op jit(solution)/shard_map/ppermute | solution.py:64
where the time goes:
time: 44.5 us; the launch traced here: 44.7 us
  blocking collectives  26.9 us (60%)
  Pallas kernels  15.7 us (35%)
  waiting for transfers between devices  1.44 us (3%)
  between operations  0.65 us (1%)
    all_to_all x1, blocking collectives, sent_to_both_twins(): lax.all_to_all(copies, axes, split_axis=0, concat_axis=0, axis_index_grou...  15.3 us
    all_to_all x1, blocking collectives, sent_directly(): lax.all_to_all(copies, exchange_axes(), split_axis=0, concat_axis=0, tile...  11.6 us
    pallas_call x1, Pallas kernels, shards(): pl.pallas_call(functools.partial(radii_kernel, blocks, pairs.shape[1], tw...  7.17 us
    pallas_call x1, Pallas kernels, shards(): pl.pallas_call(functools.partial(energy_kernel, parts, whole), out_shape=...  6.85 us
    pallas_call x1, Pallas kernels, shards(): pl.pallas_call(functools.partial(fields_kernel, blocks, atoms), out_shape...  1.69 us
    ppermute x1, waiting for transfers between devices, sent_to_both_twins(): return [here, lax.ppermute(here, 'dev', [(i, i ^ 1) for i in range(count)])]  1.44 us
  transfers between devices with their start and end apart: 1, of which 1 were waited for; matrix products, arithmetic and copies ran while one was open for 0% of the time, Pallas kernels for 0%

commit v1 on v0

--- a/solution.py
+++ b/solution.py
@@ -52,12 +52,23 @@
     return 2 - device_count % 2
 
 
+def pair_ranks(regions, device_count):
+    pairs = device_count // twin_count(device_count)
+    near = 2 - pairs % 2
+    return [
+        region * pairs + far * near + line
+        for region in reversed(range(regions))
+        for line in reversed(range(near))
+        for far in reversed(range(pairs // near))
+    ]
+
+
 def sent_to_both_twins(copies):
     count = lax.axis_size("dev")
     twins = twin_count(count)
     axes = exchange_axes()
     regions = lax.axis_size(axes) // count
-    alike = [list(reversed(range(parity, regions * count, twins))) for parity in range(twins)]
+    alike = [[pair * twins + parity for pair in pair_ranks(regions, count)] for parity in range(twins)]
     here = lax.all_to_all(copies, axes, split_axis=0, concat_axis=0, axis_index_groups=alike, tiled=True)
     if twins == 1:
         return [here]
@@ -558,9 +569,8 @@
     padded = -(-window // LANES) * LANES
     table = jax.ShapeDtypeStruct((SUBLANES + padded, LANES), jnp.int32)
     pairs_sent = copy_count // twins
-    pair_order = [
-        first + place for first in range(0, devices // twins, pairs_sent) for place in reversed(range(pairs_sent))
-    ]
+    ranks = pair_ranks(copy_count // region_devices, region_devices)
+    pair_order = [first + pair for first in range(0, devices // twins, pairs_sent) for pair in ranks]
     fields = jax.ShapeDtypeStruct((WINDOW_COUNT, window + SUBLANES, atoms), jnp.float32)
     copies, lists, window_fields = pl.pallas_call(
         functools.partial(radii_kernel, blocks, pairs.shape[1], twins, whole, pair_order),

time: 44.5 us -> 45.7 us (1.027); the launches traced: 44.7 us -> 45.1 us
  blocking collectives: 26.9 us -> 27.7 us
  Pallas kernels: 15.7 us -> 15.2 us
    pallas_call x1, Pallas kernels: 6.85 us -> 6.09 us  [shards(): pl.pallas_call(functools.partial(energy_kernel, parts, whole), out_shape=...]
where the time goes in v1:
time: 45.7 us; the launch traced here: 45.1 us
  blocking collectives  27.7 us (61%)
  Pallas kernels  15.2 us (33%)
  waiting for transfers between devices  1.44 us (3%)
  between operations  0.65 us (1%)
    all_to_all x1, blocking collectives, sent_to_both_twins(): lax.all_to_all(copies, axes, split_axis=0, concat_axis=0, axis_index_grou...  15.7 us
    all_to_all x1, blocking collectives, sent_directly(): lax.all_to_all(copies, exchange_axes(), split_axis=0, concat_axis=0, tile...  12 us
    pallas_call x1, Pallas kernels, shards(): pl.pallas_call(functools.partial(radii_kernel, blocks, pairs.shape[1], tw...  7.46 us
    pallas_call x1, Pallas kernels, shards(): pl.pallas_call(functools.partial(energy_kernel, parts, whole), out_shape=...  6.09 us
    pallas_call x1, Pallas kernels, shards(): pl.pallas_call(functools.partial(fields_kernel, blocks, atoms), out_shape...  1.69 us
    ppermute x1, waiting for transfers between devices, sent_to_both_twins(): return [here, lax.ppermute(here, 'dev', [(i, i ^ 1) for i in range(count)])]  1.44 us
  transfers between devices with their start and end apart: 1, of which 1 were waited for; matrix products, arithmetic and copies ran while one was open for 0% of the time, Pallas kernels for 0%

profile of v1, /device:TPU:0, one launch (start us, length us, event | category | flops | bytes accessed | tf_op | source)
XLA Modules:
  0.0 45.1 jit_solution(16144887965858213425)
XLA Ops:
  0.6 1.7 %shard_map.84 = f32[16,6,4,128]{3,2,1,0:T(4,128)} custom-call(f32[3,4,128]{2,1,0:T(4,128)} %refs_0_.1, s32[4,128]{1,0:T(4,128)} %refs_1_.1, f32[4,128]{1,0:T(4,128)} %refs_2_.1, s32[4,13]{1,0:T(4,128)} %refs_3_.1, s32[128]{0:T(128)} %refs_4_.1), custom_call_target="tpu_custom_call" | custom-call | tf_op jit(solution)/shard_map/pallas_call | solution.py:553
  2.3 15.7 %all_to_all.10 = f32[16,6,4,128]{3,2,1,0:T(4,128)S(1)} all-to-all(f32[16,6,4,128]{3,2,1,0:T(4,128)} %shard_map.84), channel_id=1, replica_groups={{30,26,22,18,28,24,20,16,14,10,6,2,12,8,4,0},{31,27,23,19,29,25,21,17,1..., dimensions={0} | all-to-all | bytes 393216 | tf_op jit(solution)/shard_map/all_to_all | solution.py:72
  18.0 0.0 collective-permute-start
  18.0 1.4 %collective-permute-done = f32[16,6,4,128]{3,2,1,0:T(4,128)S(1)} collective-permute-done((f32[16,6,4,128]{3,2,1,0:T(4,128)S(1)}, f32[16,6,4,128]{3,2,1,0:T(4,128)S(1)}, u32[]{:S(2)}, u32[]{:S(2)}) %collective-permute-start) | collective-permute-done | bytes 196640 | tf_op jit(solution)/shard_map/ppermute | solution.py:75
  19.5 7.5 %shard_map.85 = (f32[32,4,128]{2,1,0:T(4,128)S(1)}, s32[136,128]{1,0:T(8,128)S(1)}, f32[5,136,128]{2,1,0:T(8,128)S(1)}) custom-call(f32[16,24,128]{2,1,0:T(8,128)S(1)} %bitcast.2, f32[16,24,128]{2,1,0:T(8,128)S(1)} %bitcast.3), custom_call_target="tpu_custom_call" | custom-call | tf_op jit(solution)/shard_map/pallas_call | solution.py:575
  26.9 12.0 %all_to_all.11.gathered_ref = f32[32,4,128]{2,1,0:T(4,128)S(1)} all-to-all(f32[32,4,128]{2,1,0:T(4,128)S(1)} %get-tuple-element.9), channel_id=1, replica_groups=mesh['region'=2,'dev'=16] {'region','dev'}, dimensions={0} | all-to-all | bytes 131072 | tf_op jit(solution)/shard_map/all_to_all | solution.py:48
  39.0 6.1 %shard_map.86 = (f32[4,128]{1,0:T(4,128)}, f32[4,128]{1,0:T(4,128)}, f32[3,4,128]{2,1,0:T(4,128)}, f32[4,128]{1,0:T(4,128)}) custom-call(s32[136,128]{1,0:T(8,128)S(1)} %get-tuple-element.7.table_ref, f32[5,136,128]{2,1,0:T(8,128)S(1)} %get-tuple-element.8.window_ref, f32[32,4,128]{2,1,0:T(4,128)S(1)} %all_to_all.11.gathered_ref), custom_call_target="tpu_custom_call" | custom-call | tf_op jit(solution)/shard_map/pallas_call | solution.py:596
Async XLA Ops:
  18.0 1.4 %collective-permute-start = (f32[16,6,4,128]{3,2,1,0:T(4,128)S(1)}, f32[16,6,4,128]{3,2,1,0:T(4,128)S(1)}, u32[]{:S(2)}, u32[]{:S(2)}) collective-permute-start(f32[16,6,4,128]{3,2,1,0:T(4,128)S(1)} %all_to_all.10), channel_id=1, source_target_pairs={{0,1},{1,0},{2,3},{3,2},{4,5},{5,4},{6,7},{7,6},{8,9},{9,8},{10,11... | collective-permute-start | bytes 589832 | tf_op jit(solution)/shard_map/ppermute | solution.py:75
